TPU v7x, 32 devices: a whole 2x2x4 slice. The times are simulated.
32 devices in a mesh: ang: 16 (over z, x, core), pix: 2 (over y).
Axes of the slice: x: 2, y: 2, z: 4, core: 2. Of those that a mesh axis runs over, the one named last changes fastest.
Arguments:
- grads: bfloat16 [2, 4096, 32, 512], P(None, 'ang', 'pix')
- circle_pos: int32 [4096], replicated, may hold values from 0 to 4095, as said below
- harmonics: int32 [256], replicated, may hold values from 0 to 4095, as said below
- support: int32 [32, 512], replicated, may hold values 0 or 1
Outputs:
- update: bfloat16 [2, 4096, 32, 512], P(None, 'ang', 'pix')
- harmonic_rms: float32 [256], replicated
Inputs may be any that keep to these rules, and one draw needn't show every extreme that they name: `circle_pos`: the stored angles form 64 aligned blocks of 64 rows; block b holds the circle positions r_b + 64 * j for j = 0 to 63 in this order, and the 64 values r_b are distinct. `harmonics`: 256 distinct harmonic numbers, among them 0 and 4095.
All inputs are finite; a program needn't handle non-finite values.
Results may differ from a plain program's by a relative error of at most 0.015.
Values may be sent and summed in bfloat16 or wider, within the bound.
A program may use at most 192 MiB of HBM per device.

v0:
```python
import math

import jax
import jax.numpy as jnp
from jax import lax
from jax.sharding import PartitionSpec as P


def phase_pair(product, modulus):
    radians = (product % modulus).astype(jnp.float32) * (2.0 * math.pi / modulus)
    return (jnp.cos(radians), jnp.sin(radians))


def split_parts(value):
    if value.dtype == jnp.bfloat16:
        return (value,)
    high = value.astype(jnp.bfloat16)
    low = (value - high.astype(jnp.float32)).astype(jnp.bfloat16)
    return (high, low)


def split_einsum(form, left, right):
    left_parts = split_parts(left)
    right_parts = split_parts(right)
    total = None
    for left_rank, left_piece in enumerate(left_parts):
        for right_rank, right_piece in enumerate(right_parts):
            if left_rank + right_rank <= 1:
                term = jnp.einsum(form, left_piece, right_piece, preferred_element_type=jnp.float32)
                total = term if total is None else total + term
    return total


def normalize(coef_re, coef_im, weight, cell_count):
    square_sums = jnp.sum(weight[None, :] * (coef_re * coef_re + coef_im * coef_im), axis=1)
    totals = lax.psum(square_sums, ("ang", "pix"))
    harmonic_rms = jnp.sqrt(totals / cell_count + 1e-06)
    factor = weight[None, :] / harmonic_rms[:, None]
    return (coef_re * factor, coef_im * factor, harmonic_rms)


def direct_path(grads, circle_pos, harmonics, weight, cell_count):
    angle_count = circle_pos.shape[0]
    kept_count = harmonics.shape[0]
    moved = lax.all_to_all(grads, "ang", split_axis=2, concat_axis=1, tiled=True)
    row_local = moved.shape[2]
    col_count = moved.shape[3]
    flat = moved.reshape(2, angle_count, row_local * col_count)
    pixel_count = flat.shape[2]
    phase_cos, phase_sin = phase_pair(harmonics[:, None] * circle_pos[None, :], angle_count)
    table = jnp.concatenate((phase_cos, phase_sin), 0)
    products = split_einsum("ka,ap->kp", table, jnp.concatenate((flat[0], flat[1]), 1))
    scale = 1.0 / math.sqrt(angle_count)
    coef_re = (products[:kept_count, :pixel_count] + products[kept_count:, pixel_count:]) * scale
    coef_im = (products[:kept_count, pixel_count:] - products[kept_count:, :pixel_count]) * scale
    step_re, step_im, harmonic_rms = normalize(coef_re, coef_im, weight, cell_count)
    right_side = jnp.concatenate(
        (jnp.concatenate((step_re, -step_im), 0), jnp.concatenate((step_im, step_re), 0)), 1
    )
    synthesis = split_einsum("ka,kp->ap", table, right_side)
    scale_back = 1.0 / math.sqrt(kept_count)
    update = jnp.stack((synthesis[:, :pixel_count], synthesis[:, pixel_count:])) * scale_back
    update = update.astype(jnp.bfloat16).reshape(2, angle_count, row_local, col_count)
    return (lax.all_to_all(update, "ang", split_axis=1, concat_axis=2, tiled=True), harmonic_rms)


def body(grads, circle_pos, harmonics, support):
    ang_count = lax.axis_size("ang")
    row_pix = grads.shape[2]
    row_local = row_pix // ang_count
    col_count = grads.shape[3]
    row_start = lax.axis_index("pix") * row_pix + lax.axis_index("ang") * row_local
    weight = (
        lax.dynamic_slice_in_dim(support, row_start, row_local, 0).astype(jnp.float32).reshape(-1)
    )
    cell_count = float(row_pix * lax.axis_size("pix") * col_count)
    update, harmonic_rms = direct_path(grads, circle_pos, harmonics, weight, cell_count)
    return (update, harmonic_rms)


def solution(mesh):
    placed = (P(None, "ang", "pix", None), P(), P(), P())
    return jax.shard_map(
        body,
        mesh=mesh,
        in_specs=placed,
        out_specs=(P(None, "ang", "pix", None), P()),
        check_vma=False,
    )
```

profile of v0, /device:TPU:0, one launch (start us, length us, event | category | flops | bytes accessed | tf_op | source)
XLA Modules:
  0.0 567.8 jit_solution(330546438616177827)
XLA Ops:
  0.6 11.5 %copy.18 = bf16[2,256,16,512]{3,1,0,2:T(8,128)(2,1)} copy(bf16[2,256,16,512]{3,2,1,0:T(8,128)(2,1)} %param.4) | data formatting | bytes 16777216 | tf_op args[0]
  12.1 0.0 copy-start.6
  12.1 0.0 copy-start.8
  12.1 7.6 %all-to-all-start = ((bf16[2,256,16,512]{3,1,0,2:T(8,128)(2,1)}), bf16[2,256,16,512]{3,1,0,2:T(8,128)(2,1)}, u32[]{:S(2)}, u32[]{:S(2)}) async-start(bf16[2,256,16,512]{3,1,0,2:T(8,128)(2,1)} %copy.18), calls=%async_computation | async-start | bytes 16777216 | tf_op jit(solution)/shard_map/all_to_all | solution.py:45
  19.7 0.7 dynamic-slice_convert_fusion
  20.4 0.0 copy-done.6
  20.4 0.0 copy-done.8
  20.4 18.0 %fusion.8 = (f32[256,4096]{1,0:T(8,128)}, f32[256,4096]{1,0:T(8,128)}) fusion(s32[4096]{0:T(1024)S(1)} %copy-done.6, s32[256]{0:T(256)S(1)} %copy-done.8), kind=kLoop, calls=%fused_computation.23 | loop fusion | flops 14680064 | bytes 8406016 | tf_op jit(solution)/shard_map/cos | solution.py:11
  38.4 132.0 %all-to-all-done = bf16[2,256,16,512]{3,1,0,2:T(8,128)(2,1)} async-done(((bf16[2,256,16,512]{3,1,0,2:T(8,128)(2,1)}), bf16[2,256,16,512]{3,1,0,2:T(8,128)(2,1)}, u32[]{:S(2)}, u32[]{:S(2)}) %all-to-all-start) | async-done | bytes 8388640 | tf_op jit(solution)/shard_map/all_to_all | solution.py:45
  170.4 7.7 %copy.24 = bf16[2,256,16,512]{3,1,2,0:T(8,128)(2,1)} copy(bf16[2,256,16,512]{3,1,0,2:T(8,128)(2,1)} %all-to-all-done) | data formatting | bytes 16777216 | tf_op jit(solution)/shard_map/all_to_all | solution.py:45
  178.1 0.0 copy-start
  178.1 0.0 copy-start.2
  178.1 5.4 fusion.27
  183.4 0.0 copy-start.5
  183.4 2.1 copy-done.5
  185.6 0.0 copy-done
  185.6 1.4 copy-done.2
  187.0 8.0 %fusion.2 = f32[512,1024]{1,0:T(8,128)} fusion(bf16[4096,512]{1,0:T(8,128)(2,1)} %bitcast.21, bf16[4096,512]{1,0:T(8,128)(2,1)S(1)} %bitcast.19, f32[256,4096]{1,0:T(8,128)S(1)} %copy-done.2, f32[256,4096]{1,0:T(8,128)S(1)} %copy-done), kind=kOutput, calls=%fused_computation.15 | convolution fusion | flops 4322230272 | bytes 18874368 | tf_op jit(solution)/shard_map/ka,ap->kp/dot_general | solution.py:29
  195.0 8.5 %fusion.9 = f32[512,1024]{1,0:T(8,128)S(1)} fusion(f32[512,1024]{1,0:T(8,128)} %fusion.2, bf16[4096,512]{1,0:T(8,128)(2,1)} %bitcast.22, bf16[4096,512]{1,0:T(8,128)(2,1)} %bitcast.20, f32[256,4096]{1,0:T(8,128)S(1)} %copy-done.2, f32[256,4096]{1,0:T(8,128)S(1)} %copy-done), kind=kOutput, calls=%fused_computation.24 | convolution fusion | flops 4320657408 | bytes 20971520 | tf_op jit(solution)/shard_map/ka,ap->kp/dot_general | solution.py:29
  203.6 0.0 copy-start.4
  203.6 1.3 copy-done.4
  204.9 0.2 multiply_reduce_fusion
  205.2 72.3 %psum.7 = f32[256]{0:T(256)S(1)} all-reduce(f32[256]{0:T(256)S(1)} %multiply_reduce_fusion), channel_id=1, replica_groups=mesh['ang'=16,'pix'=2] {'ang','pix'}, use_global_device_ids=true, to_apply=%region_1.2 | all-reduce | flops 256 | bytes 2048 | tf_op jit(solution)/shard_map/psum | solution.py:36
  277.5 0.0 copy-start.7
  277.5 1.7 fusion.26
  279.3 0.0 copy-start.1
  279.3 0.0 copy-start.3
  279.3 12.7 %fusion.11 = f32[4096,1024]{1,0:T(8,128)} fusion(f32[256,512]{1,0:T(8,128)S(1)} %get-tuple-element.12, f32[256,512]{1,0:T(8,128)S(1)} %get-tuple-element.7, f32[256,512]{1,0:T(8,128)S(1)} %get-tuple-element.6, f32[256,4096]{1,0:T(8,128)} %get-tuple-element.14, f32[256,4096]{1,0:T(8,128)} %get-tuple-element.13), kind=kOutput, calls=%fused_computation.26 | convolution fusion | flops 4307025920 | bytes 26738688 | tf_op jit(solution)/shard_map/ka,kp->ap/dot_general | solution.py:29
  291.9 0.0 copy-done.7
  291.9 0.0 copy-done.1
  291.9 0.0 copy-done.3
  291.9 8.2 %fusion.19 = f32[4096,1024]{1,0:T(8,128)} fusion(f32[256,512]{1,0:T(8,128)S(1)} %get-tuple-element.12, f32[256,512]{1,0:T(8,128)S(1)} %get-tuple-element.7, f32[256,512]{1,0:T(8,128)S(1)} %get-tuple-element.6, f32[256,4096]{1,0:T(8,128)S(1)} %copy-done.3, f32[256,4096]{1,0:T(8,128)S(1)} %copy-done.1), kind=kOutput, calls=%fused_computation.39 | convolution fusion | flops 4307550208 | bytes 26738688 | tf_op jit(solution)/shard_map/ka,kp->ap/dot_general | solution.py:29
  300.1 19.3 %add_add_fusion = f32[4096,1024]{1,0:T(8,128)} fusion(f32[4096,1024]{1,0:T(8,128)} %fusion.19, f32[4096,1024]{1,0:T(8,128)} %fusion.11, f32[256,512]{1,0:T(8,128)S(1)} %get-tuple-element.12, f32[256,512]{1,0:T(8,128)S(1)} %get-tuple-element.7, f32[256,512]{1,0:T(8,128)S(1)} %get-tuple-element.6, f32[256,4096]{1,0:T(8,128)} %get-tuple-element.14, ...), kind=kOutput, calls=%fused_computation.2 | convolution fusion | flops 4318035968 | bytes 60293120 | tf_op jit(solution)/shard_map/ka,kp->ap/dot_general | solution.py:29
  319.4 6.9 %slice_bitcast_fusion.1 = (f32[1,4096,1,512]{3,1,2,0:T(8,128)S(1)}, f32[1,4096,1,512]{3,1,2,0:T(8,128)S(1)}) fusion(f32[4096,1024]{1,0:T(8,128)} %add_add_fusion), kind=kLoop, calls=%fused_computation.4 | loop fusion | bytes 33554432 | tf_op jit(solution)/shard_map/stack | solution.py:62
  326.3 2.5 fusion
  328.8 32.6 %copy.20 = bf16[2,4096,1,512]{3,0,2,1:T(2,128)(2,1)S(1)} copy(bf16[2,4096,1,512]{3,1,2,0:T(8,128)(2,1)S(1)} %fusion) | data formatting | bytes 16777216 | tf_op jit(solution)/shard_map/convert_element_type | solution.py:63
  361.4 186.9 %all_to_all.33 = bf16[2,4096,1,512]{3,0,2,1:T(2,128)(2,1)} all-to-all(bf16[2,4096,1,512]{3,0,2,1:T(2,128)(2,1)S(1)} %copy.20), channel_id=1, replica_groups=mesh['ang'=16,'pix'=2] {'ang'}, dimensions={1} | all-to-all | bytes 16777216 | tf_op jit(solution)/shard_map/all_to_all | solution.py:64
  548.3 8.0 %copy.21 = bf16[2,4096,1,512]{3,1,0,2:T(8,128)(2,1)} copy(bf16[2,4096,1,512]{3,0,2,1:T(2,128)(2,1)} %all_to_all.33) | data formatting | bytes 16777216 | tf_op jit(solution)/shard_map/all_to_all | solution.py:64
  556.2 11.5 %copy.22 = bf16[2,256,16,512]{3,2,1,0:T(8,128)(2,1)} copy(bf16[2,256,16,512]{3,1,2,0:T(8,128)(2,1)} %bitcast.18) | data formatting | bytes 16777216
  (1 shorter events, 0.0 us)
Async XLA Ops:
  12.1 8.3 %copy-start.6 = (s32[4096]{0:T(1024)S(1)}, s32[4096]{0:T(1024)}, u32[]{:S(2)}) copy-start(s32[4096]{0:T(1024)} %param.5) | copy-start | bytes 49156
  12.1 8.3 %copy-start.8 = (s32[256]{0:T(256)S(1)}, s32[256]{0:T(256)}, u32[]{:S(2)}) copy-start(s32[256]{0:T(256)} %param.6) | copy-start | bytes 3076
  12.1 158.3 %all-to-all-start = ((bf16[2,256,16,512]{3,1,0,2:T(8,128)(2,1)}), bf16[2,256,16,512]{3,1,0,2:T(8,128)(2,1)}, u32[]{:S(2)}, u32[]{:S(2)}) async-start(bf16[2,256,16,512]{3,1,0,2:T(8,128)(2,1)} %copy.18), calls=%async_computation | async-start | bytes 16777216 | tf_op jit(solution)/shard_map/all_to_all | solution.py:45
  178.1 7.5 %copy-start = (f32[256,4096]{1,0:T(8,128)S(1)}, f32[256,4096]{1,0:T(8,128)}, u32[]{:S(2)}) copy-start(f32[256,4096]{1,0:T(8,128)} %get-tuple-element.13) | copy-start | bytes 12582916
  178.1 9.0 %copy-start.2 = (f32[256,4096]{1,0:T(8,128)S(1)}, f32[256,4096]{1,0:T(8,128)}, u32[]{:S(2)}) copy-start(f32[256,4096]{1,0:T(8,128)} %get-tuple-element.14) | copy-start | bytes 12582916
  183.4 2.1 copy-start.5
  203.6 1.3 copy-start.4
  277.5 14.4 %copy-start.7 = (f32[256]{0:T(256)}, f32[256]{0:T(256)S(1)}, u32[]{:S(2)}) copy-start(f32[256]{0:T(256)S(1)} %add_sqrt_fusion) | copy-start | bytes 3076
  279.3 12.7 %copy-start.1 = (f32[256,4096]{1,0:T(8,128)S(1)}, f32[256,4096]{1,0:T(8,128)}, u32[]{:S(2)}) copy-start(f32[256,4096]{1,0:T(8,128)} %get-tuple-element.13) | copy-start | bytes 12582916
  279.3 12.7 %copy-start.3 = (f32[256,4096]{1,0:T(8,128)S(1)}, f32[256,4096]{1,0:T(8,128)}, u32[]{:S(2)}) copy-start(f32[256,4096]{1,0:T(8,128)} %get-tuple-element.14) | copy-start | bytes 12582916
where the time goes:
time: 569 us; the launch traced here: 568 us
  blocking collectives  259 us (46%)
  waiting for transfers between devices  132 us (23%)
  local copies, waits for them, and re-layouts  88.4 us (16%)
  matrix products  56.7 us (10%)
  other arithmetic  23.2 us (4%)
  starting transfers between devices  7.55 us (1%)
    all_to_all x1, blocking collectives, direct_path(): lax.all_to_all(update, 'ang', split_axis=1, concat_axis=2, tiled=True)  187 us
    all_to_all x1, waiting for transfers between devices, direct_path(): lax.all_to_all(grads, 'ang', split_axis=2, concat_axis=1, tiled=True)  132 us
    psum x1, blocking collectives, normalize(): totals = lax.psum(square_sums, ('ang', 'pix'))  72.3 us
    dot_general x5, matrix products, split_einsum(): jnp.einsum(form, left_piece, right_piece, preferred_element_type=jnp.floa...  56.7 us
    convert_element_type x1, local copies, waits for them, and re-layouts, direct_path(): update.astype(jnp.bfloat16).reshape(2, angle_count, row_local, col_count)  32.6 us
    unnamed x20, local copies, waits for them, and re-layouts  28 us
    cos x1, other arithmetic, phase_pair(): return (jnp.cos(radians), jnp.sin(radians))  18 us
  transfers between devices with their start and end apart: 1, of which 1 were waited for; matrix products, arithmetic and copies ran while one was open for 3% of the time, Pallas kernels for 0%

commit v1 on v0

v1 whole, which is shorter than its diff:
```python
import math

import jax
import jax.numpy as jnp
from jax import lax
from jax.experimental import pallas as pl
from jax.experimental.pallas import tpu as pltpu
from jax.sharding import PartitionSpec as P


def phase_table(harmonics, positions, modulus):
    radians = ((harmonics[:, None] * positions[None, :]) % modulus).astype(jnp.float32) * (2.0 * math.pi / modulus)
    cos, sin = jnp.cos(radians), jnp.sin(radians)
    return jnp.concatenate((jnp.concatenate((cos, sin), 1), jnp.concatenate((-sin, cos), 1)), 0)


def split_parts(value):
    high = lax.reduce_precision(value, 8, 7)
    return (high.astype(jnp.bfloat16), (value - high).astype(jnp.bfloat16))


def table_einsum(form, table, right):
    return sum(
        jnp.einsum(form, piece, right, preferred_element_type=jnp.float32) for piece in split_parts(table)
    )


def body(grads, circle_pos, harmonics, support):
    ang_count = lax.axis_size("ang")
    angle_local, row_pix, col_count = grads.shape[1:]
    row_local = row_pix // ang_count
    angle_count = circle_pos.shape[0]
    kept_count = harmonics.shape[0]
    me = lax.axis_index("ang")
    row_start = lax.axis_index("pix") * row_pix + me * row_local
    weight = lax.dynamic_slice_in_dim(support, row_start, row_local, 0).astype(jnp.float32)
    cell_count = float(row_pix * lax.axis_size("pix") * col_count)
    positions = lax.dynamic_slice_in_dim(circle_pos, me * angle_local, angle_local, 0)
    table = phase_table(harmonics, positions, angle_count)
    flat = grads.reshape(2 * angle_local, row_pix, col_count)
    partial = table_einsum("ka,arc->rkc", table, flat)
    coef = lax.psum_scatter(partial, "ang", scatter_dimension=0, tiled=True)
    coef = coef * (weight[:, None, :] * (1.0 / math.sqrt(angle_count)))
    squares = jnp.sum(coef * coef, axis=(0, 2))
    totals = lax.psum(squares[:kept_count] + squares[kept_count:], ("ang", "pix"))
    harmonic_rms = jnp.sqrt(totals / cell_count + 1e-06)
    every = lax.all_gather(coef.astype(jnp.bfloat16), "ang", axis=0, tiled=True)
    scale = (1.0 / math.sqrt(kept_count)) / harmonic_rms
    back = table * jnp.concatenate((scale, scale))[:, None]
    update = table_einsum("ka,rkc->arc", back, every).astype(jnp.bfloat16)
    return (update.reshape(grads.shape), harmonic_rms)


MESH = pl.DeviceIdType.MESH
ORDER = ((1, 3, 0), (1, 0, 0), (0, 3, 1), (0, 0, 1), (1, 3, 1), (1, 0, 1),
         (1, 2, 0), (1, 1, 0), (0, 2, 1), (0, 1, 1), (1, 2, 1), (1, 1, 1))


def starts():
    up, down, result = 0, 0, {}
    for half, t, rel in ORDER:
        result[half, t, rel] = (up, down)
        up += t > 0
        down += t < 3
    return result


def item_of(half, t, rel):
    return t if half == 0 else 4 + 2 * t + rel


def reduce_gather(grads_ref, high_ref, low_ref, weight_ref, out_ref, total_ref,
                  core_out, core_in, held, x_out, x_in, z_out, z_in, b_out, b_in, gathered, squares, y_in,
                  core_send, core_recv, x_send, x_recv, z_send, z_recv, b_send, b_recv,
                  gather_send, gather_recv, out_sem, y_send, y_recv):
    me = lax.axis_index("ang")
    pix = lax.axis_index("pix")
    z, x, c = me // 4, (me // 2) % 2, me % 2
    sibling = (z * 4 + x * 2 + 1 - c, pix)
    beside = (z * 4 + (1 - x) * 2 + c, pix)
    across = (me, 1 - pix)

    barrier = pltpu.get_barrier_semaphore()
    for device in (sibling, beside, across):
        pl.semaphore_signal(barrier, inc=1, device_id=device, device_id_type=MESH)

    @pl.when(z < 3)
    def _():
        pl.semaphore_signal(barrier, inc=1, device_id=(me + 4, pix), device_id_type=MESH)

    @pl.when(z > 0)
    def _():
        pl.semaphore_signal(barrier, inc=1, device_id=(me - 4, pix), device_id_type=MESH)

    inner = (z > 0) & (z < 3)

    @pl.when(inner)
    def _():
        pl.semaphore_wait(barrier, 5)

    @pl.when(jnp.logical_not(inner))
    def _():
        pl.semaphore_wait(barrier, 4)

    def unit(half, t, rel, own):
        xx = x if rel else 1 - x
        cc = c if own else 1 - c
        return (t * 4 + xx * 2 + cc) * 2 + half

    def remote(src, dst, send, recv, device):
        return pltpu.make_async_remote_copy(
            src_ref=src, dst_ref=dst, send_sem=send, recv_sem=recv, device_id=device, device_id_type=MESH)

    def core_copy(j):
        return remote(core_out.at[j], core_in.at[j], core_send.at[j], core_recv.at[j], sibling)

    def x_copy(t):
        return remote(x_out.at[t], x_in.at[t], x_send.at[t], x_recv.at[t], beside)

    def lanes(half):
        return pl.ds(half * 256, 256)

    def out_copy(u, half):
        return pltpu.make_async_copy(gathered.at[u], out_ref.at[u // 2, :, lanes(half)], out_sem.at[u])

    def partial(u, half):
        value = grads_ref[u // 2, :, lanes(half)]
        return (jnp.dot(high_ref[...], value, preferred_element_type=jnp.float32)
                + jnp.dot(low_ref[...], value, preferred_element_type=jnp.float32))

    def nth(i):
        return (i % 2) * (i // 2) + (1 - i % 2) * (3 - i // 2)

    def send_core(half, rel):
        @pl.loop(0, 4)
        def _(i):
            t = nth(i)
            j = (t * 2 + rel) * 2 + half
            core_out[j] = partial(unit(half, t, rel, False), half).astype(jnp.bfloat16)
            core_copy(j).start()

    def keep(half, rel):
        @pl.loop(0, 4)
        def _(i):
            t = nth(i)
            j = (t * 2 + rel) * 2 + half
            value = partial(unit(half, t, rel, True), half)
            core_copy(j).wait_recv()
            value = value + core_in[j].astype(jnp.float32)
            if half == 0 and rel == 0:
                x_out[t] = value.astype(jnp.bfloat16)
                x_copy(t).start()
            else:
                held[item_of(half, t, rel)] = value

    send_core(0, 0)
    send_core(1, 0)
    keep(0, 0)
    keep(1, 0)
    send_core(0, 1)
    send_core(1, 1)
    keep(0, 1)
    keep(1, 1)

    squares[...] = jnp.zeros_like(squares)

    def at_hand(u, half):
        out_copy(u, half).start()

        @pl.loop(0, 8)
        def _(i):
            rows = pl.ds(pl.multiple_of(i * 32, 32), 32)
            lower = pl.ds(pl.multiple_of(i * 32 + 256, 32), 32)
            re = gathered[u, rows, :].astype(jnp.float32)
            im = gathered[u, lower, :].astype(jnp.float32)
            both = re * re + im * im
            squares[rows, :] += both[:, :128] + both[:, 128:]

    def add_up(target, at, sources, weight):
        @pl.loop(0, 16)
        def _(i):
            rows = pl.ds(pl.multiple_of(i * 32, 32), 32)
            value = None
            for ref, index in sources:
                term = ref[index + (rows, slice(None))].astype(jnp.float32)
                value = term if value is None else value + term
            if weight is not None:
                value = value * weight_ref[weight]
            target[at, rows, :] = value.astype(jnp.bfloat16)

    begin = starts()

    def run(zz):
        sent = []
        events = []

        def z_copy(k, way):
            return remote(z_out.at[k], z_in.at[way, k], z_send.at[k], z_recv.at[way, k],
                          (me + 4 if way == 0 else me - 4, pix))

        def b_copy():
            return remote(b_out.at[0], b_in.at[0], b_send.at[0], b_recv.at[0], beside)

        def gather_copy(u, way):
            device = (None, None, beside, sibling)[way] or (me + 4 if way == 0 else me - 4, pix)
            return remote(gathered.at[u], gathered.at[u], gather_send.at[way, u], gather_recv.at[u], device)

        def arrive(u):
            gather_copy(u, 3).wait_recv()

        def start(copy):
            copy.start()
            sent.append(copy)

        def onward(u, ways):
            for way in ways:
                start(gather_copy(u, way))

        def z_sources(half, t, rel):
            k = item_of(half, t, rel)
            sources = [(held, (k,))]
            if half == 0:
                x_copy(t).wait_recv()
                sources.append((x_in, (t,)))
            if zz > 0 and t >= zz:
                z_copy(k, 0).wait_recv()
                sources.append((z_in, (0, k)))
            if zz < 3 and t <= zz:
                z_copy(k, 1).wait_recv()
                sources.append((z_in, (1, k)))
            return sources

        def away(t):
            ways = []
            if zz < 3 and t <= zz:
                ways.append(0)
            if zz > 0 and t >= zz:
                ways.append(1)
            return ways

        def pass_on(half, t, rel):
            k = item_of(half, t, rel)
            add_up(z_out, k, z_sources(half, t, rel), None)
            start(z_copy(k, 0 if t > zz else 1))

        def cross():
            add_up(b_out, 0, z_sources(1, zz, 0), None)
            start(b_copy())

        def finish(half):
            sources = z_sources(half, zz, 1)
            if half == 1:
                b_copy().wait_recv()
                sources.append((b_in, (0,)))
            u = unit(half, zz, 1, True)
            add_up(gathered, u, sources, u)
            onward(u, [2] + away(zz) + [3])
            at_hand(u, half)

        def forward(half, t, rel, ways):
            u = unit(half, t, rel, True)
            arrive(u)
            onward(u, ways + [3])
            at_hand(u, half)

        def from_core(half, t, rel):
            u = unit(half, t, rel, False)
            arrive(u)
            at_hand(u, half)

        def put(step, rank, action, *args):
            events.append((step, rank, len(events), action, args))

        def got(step, half, t, rel):
            put(step + 2, 3, from_core, half, t, rel)

        ends = {}
        for half, t, rel in ORDER:
            up, down = begin[half, t, rel]
            ends[half, t, rel] = max(up + t if t > 0 else 0, down + 3 - t if t < 3 else 0)
            if t != zz:
                put(up + zz if t > zz else down + 3 - zz, 0, pass_on, half, t, rel)
        for t in range(4):
            far = abs(zz - t)
            step = ends[0, t, 1]
            if far == 0:
                put(step, 1, finish, 0)
            else:
                put(step + far, 1, forward, 0, t, 1, [2] + away(t))
            got(step + far, 0, t, 1)
            put(step + far + 1, 2, forward, 0, t, 0, [])
            got(step + far + 1, 0, t, 0)
            step = max(ends[1, t, 1], ends[1, t, 0] + 1)
            if far == 0:
                put(ends[1, t, 0], 0, cross)
                put(step, 1, finish, 1)
            else:
                put(step + far, 1, forward, 1, t, 1, away(t))
            got(step + far, 1, t, 1)
            put(step + far + 1, 1, forward, 1, t, 0, away(t))
            got(step + far + 1, 1, t, 0)
        for event in sorted(events, key=lambda entry: entry[:3]):
            event[3](*event[4])
        for copy in sent:
            copy.wait_send()

    for zz in range(4):
        pl.when(z == zz)(lambda zz=zz: run(zz))

    y_copy = remote(squares, y_in, y_send, y_recv, across)
    y_copy.start()

    @pl.loop(0, 16)
    def _(j):
        core_copy(j).wait_send()

    @pl.loop(0, 4)
    def _(t):
        x_copy(t).wait_send()

    @pl.loop(0, 16)
    def _(r):
        out_copy(2 * r, 0).wait()
        out_copy(2 * r + 1, 1).wait()

    y_copy.wait()
    total_ref[...] = squares[...] + y_in[...]


def gathered_coefficients(units, table, weight):
    high, low = split_parts(table)
    rows, cols = units.shape[1], units.shape[2] // 2
    block = lambda n: pltpu.VMEM((n, rows, cols), jnp.bfloat16)
    dma = pltpu.SemaphoreType.DMA
    vmem = pl.BlockSpec(memory_space=pltpu.VMEM)
    return pl.pallas_call(
        reduce_gather,
        out_shape=(jax.ShapeDtypeStruct(units.shape, jnp.bfloat16),
                   jax.ShapeDtypeStruct((rows // 2, 128), jnp.float32)),
        in_specs=[vmem] * 4,
        out_specs=(pl.BlockSpec(memory_space=pl.ANY), vmem),
        scratch_shapes=[
            block(16), block(16), pltpu.VMEM((12, rows, cols), jnp.float32), block(4), block(4),
            block(12), pltpu.VMEM((2, 12, rows, cols), jnp.bfloat16), block(1), block(1), block(32),
            pltpu.VMEM((rows // 2, 128), jnp.float32), pltpu.VMEM((rows // 2, 128), jnp.float32),
            dma((16,)), dma((16,)), dma((4,)), dma((4,)), dma((12,)), dma((2, 12)), dma((1,)), dma((1,)),
            dma((4, 32)), dma((32,)), dma((32,)), dma, dma,
        ],
        compiler_params=pltpu.CompilerParams(
            collective_id=0, has_side_effects=True, vmem_limit_bytes=58 * 2**20),
    )(units, high, low, weight)


def kernel_path(grads, circle_pos, harmonics, support):
    angle_local, row_pix, col_count = grads.shape[1:]
    angle_count = circle_pos.shape[0]
    kept_count = harmonics.shape[0]
    halves, lanes = 2, col_count // 2
    me = lax.axis_index("ang")
    positions = lax.dynamic_slice_in_dim(circle_pos, me * angle_local, angle_local, 0)
    table = phase_table(harmonics, positions, angle_count)
    units = grads.reshape(2 * angle_local, row_pix, col_count).transpose(1, 0, 2)
    weight = lax.dynamic_slice_in_dim(support, lax.axis_index("pix") * row_pix, row_pix, 0).astype(jnp.float32)
    weight = (weight * (1.0 / math.sqrt(angle_count))).reshape(row_pix * halves, 1, lanes)
    every, squares = gathered_coefficients(units, table, weight)
    cell_count = float(row_pix * lax.axis_size("pix") * col_count)
    harmonic_rms = jnp.sqrt(jnp.sum(squares, axis=1) / cell_count + 1e-06)
    scale = (1.0 / math.sqrt(kept_count)) / harmonic_rms
    back = table * jnp.concatenate((scale, scale))[:, None]
    update = jnp.einsum("ka,rkc->arc", back.astype(jnp.bfloat16), every, preferred_element_type=jnp.float32)
    return (update.astype(jnp.bfloat16).reshape(grads.shape), harmonic_rms)


def chosen(grads, circle_pos, harmonics, support):
    sizes = (lax.axis_size("ang"), lax.axis_size("pix"), harmonics.shape[0]) + grads.shape[1:]
    fits = sizes == (16, 2, 256, 256, 16, 512)
    return (kernel_path if fits else body)(grads, circle_pos, harmonics, support)


def solution(mesh):
    return jax.shard_map(
        chosen,
        mesh=mesh,
        in_specs=(P(None, "ang", "pix", None), P(), P(), P()),
        out_specs=(P(None, "ang", "pix", None), P()),
        check_vma=False,
    )
```

time: 569 us -> 177 us (0.31)
  blocking collectives: 259 us -> 0 us
  Pallas kernels: 0 us -> 136 us
  waiting for transfers between devices: 132 us -> 0 us
  local copies, waits for them, and re-layouts: 88.4 us -> 24.4 us
  matrix products: 56.7 us -> 10.8 us
  other arithmetic: 23.2 us -> 5.33 us
  starting transfers between devices: 7.55 us -> 0 us
    all_to_all x1 -> x0, blocking collectives: 187 us -> none  [direct_path(): lax.all_to_all(update, 'ang', split_axis=1, concat_axis=2, tiled=True)]
    pallas_call x0 -> x1, Pallas kernels: none -> 136 us  [gathered_coefficients(): pl.pallas_call(reduce_gather, out_shape=(jax.ShapeDtypeStruct(units.shape...]
    all_to_all x1 -> x0, waiting for transfers between devices: 132 us -> none  [direct_path(): lax.all_to_all(grads, 'ang', split_axis=2, concat_axis=1, tiled=True)]
    psum x1 -> x0, blocking collectives: 72.3 us -> none  [normalize(): totals = lax.psum(square_sums, ('ang', 'pix'))]
    dot_general x5 -> x1, matrix products: 56.7 us -> 10.8 us  [kernel_path(): jnp.einsum('ka,rkc->arc', back.astype(jnp.bfloat16), every, preferred_ele...]
    convert_element_type x1 -> x0, local copies, waits for them, and re-layouts: 32.6 us -> none  [direct_path(): update.astype(jnp.bfloat16).reshape(2, angle_count, row_local, col_count)]
    cos x1 -> x0, other arithmetic: 18 us -> none  [phase_pair(): return (jnp.cos(radians), jnp.sin(radians))]
    all_to_all x2 -> x0, local copies, waits for them, and re-layouts: 15.6 us -> none  [the longest x1 7.96 us: direct_path(): lax.all_to_all(update, 'ang', split_axis=1, concat_axis=2, tiled=True)]
  transfers between devices with their start and end apart: 1 -> 0, of which waited for: 1 -> 0; matrix products, arithmetic and copies ran while one was open for 3% -> 0% of each run, Pallas kernels for 0% -> 0%
where the time goes in v1:
time: 177 us
  Pallas kernels  136 us (77%)
  local copies, waits for them, and re-layouts  24.4 us (14%)
  matrix products  10.8 us (6%)
  other arithmetic  5.33 us (3%)
    pallas_call x1, Pallas kernels, gathered_coefficients(): pl.pallas_call(reduce_gather, out_shape=(jax.ShapeDtypeStruct(units.shape...  136 us
    unnamed x2, local copies, waits for them, and re-layouts  23 us
    dot_general x1, matrix products, kernel_path(): jnp.einsum('ka,rkc->arc', back.astype(jnp.bfloat16), every, preferred_ele...  10.8 us

profile of v1, /device:TPU:0, one launch (start us, length us, event | category | flops | bytes accessed | tf_op | source)
XLA Modules:
  0.0 176.9 jit_solution(3147375600060258397)
XLA Ops:
  0.6 0.8 dynamic_slice.6
  1.4 0.8 convert_multiply_fusion
  2.2 0.6 reshape.17.weight_ref
  2.8 1.8 %fusion.7 = (f32[256,256]{1,0:T(8,128)S(1)}, f32[256,256]{1,0:T(8,128)S(1)}, f32[256,256]{1,0:T(8,128)S(1)}) fusion(s32[256]{0:T(256)S(1)} %dynamic_slice.6, s32[256]{0:T(256)} %param.6), kind=kLoop, calls=%fused_computation.16 | loop fusion | flops 983040 | bytes 788480 | tf_op jit(solution)/shard_map/sin | solution.py:13
  4.6 1.2 fusion
  5.8 11.5 %copy.6 = bf16[2,256,16,512]{3,1,0,2:T(8,128)(2,1)} copy(bf16[2,256,16,512]{3,2,1,0:T(8,128)(2,1)} %param.4) | data formatting | bytes 16777216 | tf_op args[0]
  17.3 135.6 %shard_map.59 = (bf16[16,512,512]{2,1,0:T(8,128)(2,1)}, f32[256,128]{1,0:T(8,128)}) custom-call(bf16[16,512,512]{2,1,0:T(8,128)(2,1)} %bitcast.8, bf16[512,512]{1,0:T(8,128)(2,1)} %get-tuple-element.11.high_ref, bf16[512,512]{1,0:T(8,128)(2,1)} %get-tuple-element.10.low_ref, f32[32,1,256]{2,1,0:T(1,128)} %reshape.17.weight_ref), custom_call_target="tpu_custom_call" | custom-call | tf_op jit(solution)/shard_map/pallas_call | solution.py:336
  152.9 1.0 reduce_sum.9
  154.0 0.6 broadcast_divide_fusion
  154.6 10.8 %convolution_convert_fusion = bf16[512,16,512]{2,0,1:T(8,128)(2,1)} fusion(bf16[16,512,512]{2,1,0:T(8,128)(2,1)} %get-tuple-element.5, f32[512]{0:T(512)S(1)} %pad_maximum_fusion, f32[256,256]{1,0:T(8,128)S(1)} %get-tuple-element.14, f32[256,256]{1,0:T(8,128)S(1)} %get-tuple-element.13, f32[256,256]{1,0:T(8,128)S(1)} %get-tuple-element.12), kind=kOutput, calls=%fused_computation | convolution fusion | flops 4300472320 | bytes 17565696 | tf_op jit(solution)/shard_map/ka,rkc->arc/dot_general | solution.py:370
  165.4 11.5 %copy.8 = bf16[2,256,16,512]{3,2,1,0:T(8,128)(2,1)} copy(bf16[2,256,16,512]{3,1,0,2:T(8,128)(2,1)} %bitcast.9) | data formatting | bytes 16777216
  (1 shorter events, 0.0 us)

commit v2 on v1

--- a/solution.py
+++ b/solution.py
@@ -123,6 +123,10 @@
     def out_copy(u, half):
         return pltpu.make_async_copy(gathered.at[u], out_ref.at[u // 2, :, lanes(half)], out_sem.at[u])
 
+    def z_copy(k, way):
+        return remote(z_out.at[k], z_in.at[way, k], z_send.at[k], z_recv.at[way, k],
+                      (me + 4 if way == 0 else me - 4, pix))
+
     def partial(u, half):
         value = grads_ref[u // 2, :, lanes(half)]
         return (jnp.dot(high_ref[...], value, preferred_element_type=jnp.float32)
@@ -152,15 +156,27 @@
                 x_copy(t).start()
             else:
                 held[item_of(half, t, rel)] = value
-
+            if half == 1:
+                k = item_of(half, t, rel)
+
+                @pl.when((z == 0) & (t > 0))
+                def _():
+                    z_out[k] = value.astype(jnp.bfloat16)
+                    z_copy(k, 0).start()
+
+                @pl.when((z == 3) & (t < 3))
+                def _():
+                    z_out[k] = value.astype(jnp.bfloat16)
+                    z_copy(k, 1).start()
+
+    send_core(1, 0)
     send_core(0, 0)
-    send_core(1, 0)
+    keep(1, 0)
     keep(0, 0)
-    keep(1, 0)
+    send_core(1, 1)
+    keep(1, 1)
     send_core(0, 1)
-    send_core(1, 1)
     keep(0, 1)
-    keep(1, 1)
 
     squares[...] = jnp.zeros_like(squares)
 
@@ -193,10 +209,6 @@
     def run(zz):
         sent = []
         events = []
-
-        def z_copy(k, way):
-            return remote(z_out.at[k], z_in.at[way, k], z_send.at[k], z_recv.at[way, k],
-                          (me + 4 if way == 0 else me - 4, pix))
 
         def b_copy():
             return remote(b_out.at[0], b_in.at[0], b_send.at[0], b_recv.at[0], beside)
@@ -278,7 +290,9 @@
         for half, t, rel in ORDER:
             up, down = begin[half, t, rel]
             ends[half, t, rel] = max(up + t if t > 0 else 0, down + 3 - t if t < 3 else 0)
-            if t != zz:
+            if half == 1 and t != zz and zz in (0, 3):
+                sent.append(z_copy(item_of(half, t, rel), 0 if zz == 0 else 1))
+            elif t != zz:
                 put(up + zz if t > zz else down + 3 - zz, 0, pass_on, half, t, rel)
         for t in range(4):
             far = abs(zz - t)
@@ -351,6 +365,59 @@
     )(units, high, low, weight)
 
 
+def rows_first(grads_ref, units_ref, spread):
+    angles, rows, cols = grads_ref.shape
+    for lane in range(cols // 128):
+        span = slice(lane * 128, lane * 128 + 128)
+        spread[lane] = grads_ref[:, :, span].astype(jnp.float32).reshape(angles * rows, 128)
+        for row in range(rows):
+            units_ref[row, :, span] = spread[lane, pl.ds(row, angles, stride=rows), :].astype(jnp.bfloat16)
+
+
+def by_rows(flat):
+    angles, rows, cols = flat.shape
+    block = 128
+    return pl.pallas_call(
+        rows_first,
+        grid=(angles // block,),
+        out_shape=jax.ShapeDtypeStruct((rows, angles, cols), jnp.bfloat16),
+        in_specs=[pl.BlockSpec((block, rows, cols), lambda i: (i, 0, 0))],
+        out_specs=pl.BlockSpec((rows, block, cols), lambda i: (0, i, 0)),
+        scratch_shapes=[pltpu.VMEM((cols // 128, block * rows, 128), jnp.float32)],
+        compiler_params=pltpu.CompilerParams(vmem_limit_bytes=40 * 2**20),
+    )(flat)
+
+
+def synthesis(back_ref, every_ref, update_ref, spread):
+    angles, rows, cols = update_ref.shape
+
+    @pl.loop(0, rows)
+    def _(row):
+        value = jnp.dot(back_ref[...], every_ref[row], preferred_element_type=jnp.float32)
+        for lane in range(cols // 128):
+            spread[lane, pl.ds(row, angles, stride=rows), :] = value[:, lane * 128:lane * 128 + 128]
+
+    for lane in range(cols // 128):
+        span = slice(lane * 128, lane * 128 + 128)
+        update_ref[:, :, span] = spread[lane].reshape(angles, rows, 128).astype(jnp.bfloat16)
+
+
+def synthesized(back, every):
+    angles, depth = back.shape
+    rows, _, cols = every.shape
+    block = 256
+    return pl.pallas_call(
+        synthesis,
+        grid=(angles // block,),
+        out_shape=jax.ShapeDtypeStruct((angles, rows, cols), jnp.bfloat16),
+        in_specs=[pl.BlockSpec((block, depth), lambda i: (i, 0)),
+                  pl.BlockSpec((rows, depth, cols), lambda i: (0, 0, 0))],
+        out_specs=pl.BlockSpec((block, rows, cols), lambda i: (i, 0, 0)),
+        scratch_shapes=[pltpu.VMEM((cols // 128, block * rows, 128), jnp.float32)],
+        compiler_params=pltpu.CompilerParams(vmem_limit_bytes=50 * 2**20),
+    )(back, every)
+
+
 def kernel_path(grads, circle_pos, harmonics, support):
     angle_local, row_pix, col_count = grads.shape[1:]
     angle_count = circle_pos.shape[0]
@@ -359,7 +426,7 @@
     me = lax.axis_index("ang")
     positions = lax.dynamic_slice_in_dim(circle_pos, me * angle_local, angle_local, 0)
     table = phase_table(harmonics, positions, angle_count)
-    units = grads.reshape(2 * angle_local, row_pix, col_count).transpose(1, 0, 2)
+    units = by_rows(grads.reshape(2 * angle_local, row_pix, col_count))
     weight = lax.dynamic_slice_in_dim(support, lax.axis_index("pix") * row_pix, row_pix, 0).astype(jnp.float32)
     weight = (weight * (1.0 / math.sqrt(angle_count))).reshape(row_pix * halves, 1, lanes)
     every, squares = gathered_coefficients(units, table, weight)
@@ -367,8 +434,8 @@
     harmonic_rms = jnp.sqrt(jnp.sum(squares, axis=1) / cell_count + 1e-06)
     scale = (1.0 / math.sqrt(kept_count)) / harmonic_rms
     back = table * jnp.concatenate((scale, scale))[:, None]
-    update = jnp.einsum("ka,rkc->arc", back.astype(jnp.bfloat16), every, preferred_element_type=jnp.float32)
-    return (update.astype(jnp.bfloat16).reshape(grads.shape), harmonic_rms)
+    update = synthesized(back.T.astype(jnp.bfloat16), every)
+    return (update.reshape(grads.shape), harmonic_rms)
 
 
 def chosen(grads, circle_pos, harmonics, support):

time: 177 us -> 192 us (1.085)
  Pallas kernels: 136 us -> 179 us
  local copies, waits for them, and re-layouts: 24.4 us -> 6.93 us
  matrix products: 10.8 us -> 0 us
    pallas_call x0 -> x2, Pallas kernels: none -> 31.9 us  [the longest x1 22.9 us: synthesized(): pl.pallas_call(synthesis, grid=(angles // block,), out_shape=jax.ShapeDty...]
    unnamed x2, local copies, waits for them, and re-layouts: 23 us -> 3.39 us
    pallas_call x1, Pallas kernels: 136 us -> 147 us  [gathered_coefficients(): pl.pallas_call(reduce_gather, out_shape=(jax.ShapeDtypeStruct(units.shape...]
    dot_general x1 -> x0, matrix products: 10.8 us -> none  [kernel_path(): jnp.einsum('ka,rkc->arc', back.astype(jnp.bfloat16), every, preferred_ele...]
    convert_element_type x0 -> x2, local copies, waits for them, and re-layouts: none -> 2.12 us  [split_parts(): return (high.astype(jnp.bfloat16), (value - high).astype(jnp.bfloat16))]
where the time goes in v2:
time: 192 us; the launch traced here: 191 us
  Pallas kernels  179 us (93%)
  local copies, waits for them, and re-layouts  6.93 us (4%)
  other arithmetic  4.36 us (2%)
    pallas_call x1, Pallas kernels, gathered_coefficients(): pl.pallas_call(reduce_gather, out_shape=(jax.ShapeDtypeStruct(units.shape...  147 us
    pallas_call x1, Pallas kernels, synthesized(): pl.pallas_call(synthesis, grid=(angles // block,), out_shape=jax.ShapeDty...  22.9 us
    pallas_call x1, Pallas kernels, by_rows(): pl.pallas_call(rows_first, grid=(angles // block,), out_shape=jax.ShapeDt...  9.01 us

profile of v2, /device:TPU:0, one launch (start us, length us, event | category | flops | bytes accessed | tf_op | source)
XLA Modules:
  0.0 191.3 jit_solution(14346171849342593167)
XLA Ops:
  0.6 0.8 dynamic_slice.6
  1.4 0.8 convert_multiply_fusion
  2.2 0.7 reshape.17.weight_ref
  2.8 1.8 fusion.5
  4.6 0.1 fusion
  4.8 1.1 copy.7.low_ref
  5.8 1.1 copy.6.high_ref
  6.9 9.0 %shard_map.59.grads_ref = bf16[16,512,512]{2,1,0:T(8,128)(2,1)S(1)} custom-call(bf16[512,16,512]{2,1,0:T(8,128)(2,1)} %bitcast.4), custom_call_target="tpu_custom_call" | custom-call | tf_op jit(solution)/shard_map/pallas_call | solution.py:380
  15.9 0.0 copy-start
  15.9 3.4 %copy-done = bf16[16,512,512]{2,1,0:T(8,128)(2,1)} copy-done((bf16[16,512,512]{2,1,0:T(8,128)(2,1)}, bf16[16,512,512]{2,1,0:T(8,128)(2,1)S(1)}, u32[]{:S(2)}) %copy-start) | copy-done | bytes 8388632
  19.3 147.5 %shard_map.60 = (bf16[16,512,512]{2,1,0:T(8,128)(2,1)}, f32[256,128]{1,0:T(8,128)}) custom-call(bf16[16,512,512]{2,1,0:T(8,128)(2,1)} %copy-done, bf16[512,512]{1,0:T(8,128)(2,1)} %copy.6.high_ref, bf16[512,512]{1,0:T(8,128)(2,1)} %copy.7.low_ref, f32[32,1,256]{2,1,0:T(1,128)} %reshape.17.weight_ref), custom_call_target="tpu_custom_call" | custom-call | tf_op jit(solution)/shard_map/pallas_call | solution.py:350
  166.8 1.0 reduce_sum.9
  167.8 0.6 broadcast_divide_fusion
  168.4 0.1 fusion.1.back_ref
  168.4 22.9 %shard_map.61 = bf16[512,16,512]{2,1,0:T(8,128)(2,1)} custom-call(bf16[512,512]{1,0:T(8,128)(2,1)S(1)} %fusion.1.back_ref, bf16[16,512,512]{2,1,0:T(8,128)(2,1)} %get-tuple-element.5.every_ref), custom_call_target="tpu_custom_call" | custom-call | tf_op jit(solution)/shard_map/pallas_call | solution.py:409
  (1 shorter events, 0.0 us)
Async XLA Ops:
  15.9 3.4 %copy-start = (bf16[16,512,512]{2,1,0:T(8,128)(2,1)}, bf16[16,512,512]{2,1,0:T(8,128)(2,1)S(1)}, u32[]{:S(2)}) copy-start(bf16[16,512,512]{2,1,0:T(8,128)(2,1)S(1)} %shard_map.59.grads_ref) | copy-start | bytes 25165828
